TPU v7x, 32 devices: a whole 2x2x4 slice. The times are simulated.
32 devices in a mesh: groups: 2 (over x), band: 16 (over z, y, core).
Axes of the slice: x: 2, y: 2, z: 4, core: 2. Of those that a mesh axis runs over, the one named last changes fastest.
Arguments:
- factor: bfloat16 [32768, 128], P(('groups', 'band')), parts along dimension 0
- near_vals: bfloat16 [512, 5, 64, 64], P(('groups', 'band')), parts along dimension 0, may hold values from 0.049804688 to 4
- far_vals: bfloat16 [32768, 512], P(('groups', 'band')), parts along dimension 0, may hold values from 0.049804688 to 4
- pub_rows: int32 [32, 32], P(('groups', 'band')), parts along dimension 0, may hold values from 0 to 1023
- far_count: int32 [32, 16], P(('groups', 'band')), parts along dimension 0, may hold values from 1 to 32, as said below
Outputs:
- updated: float32 [32768, 128], P(('groups', 'band')), parts along dimension 0
There are 2 independent parts, one for each index of `groups`. A program takes and returns all parts, laid end to end along the dimension named above; each array names one. Nothing has to cross between parts.
Inputs may be any that keep to these rules, and one draw needn't show every extreme that they name: `far_count`: in every row some entry equals 32.
All inputs are finite; a program needn't handle non-finite values.
Results may differ from a plain program's by a relative error of at most 0.0003.
Values may be sent and summed in bfloat16 or wider, within the bound.
A program may use at most 64 MiB of HBM per device.

v0:
```python
import jax
import jax.numpy as jnp
from jax import lax
from jax.sharding import PartitionSpec as P

BLOCK = 64
HALF_BLOCKS = 2


def extended(shard, sides, width):
    for axis, dim in sides:
        peers, length = (lax.axis_size(axis), shard.shape[dim])
        up = [(i, (i + 1) % peers) for i in range(peers - 1)]
        down = [(j, i) for i, j in up]
        last = lax.slice_in_dim(shard, length - width, length, axis=dim)
        first = lax.slice_in_dim(shard, 0, width, axis=dim)
        before = lax.ppermute(last, axis, up)
        after = lax.ppermute(first, axis, down)
        shard = jnp.concatenate([before, shard, after], axis=dim)
    return shard


def shards(factor, near_vals, far_vals, pub_rows, far_count):
    row_count, rank_width = factor.shape
    band_size = lax.axis_size("band")
    margin = HALF_BLOCKS * BLOCK
    padded = extended(factor, (("band", 0),), margin)
    block_count = row_count // BLOCK
    blocks = padded.reshape(block_count + 2 * HALF_BLOCKS, BLOCK, rank_width)
    near_sum = jnp.zeros((block_count, BLOCK, rank_width), jnp.float32)
    for offset in range(2 * HALF_BLOCKS + 1):
        near_sum = near_sum + jnp.einsum(
            "bij,bjk->bik",
            near_vals[:, offset],
            blocks[offset : offset + block_count],
            preferred_element_type=jnp.float32,
        )
    near_sum = near_sum.reshape(row_count, rank_width)
    slot_count = pub_rows.shape[1]
    chosen = jnp.take(factor, pub_rows[0], axis=0)
    slot_index = jnp.arange(band_size * slot_count, dtype=jnp.int32) % slot_count
    live_slots = slot_index < jnp.repeat(far_count[0], slot_count)
    masked = jnp.where(live_slots[None, :], far_vals, jnp.zeros((), far_vals.dtype))
    own_gram = lax.dot_general(
        factor, factor, (((0,), (0,)), ((), ())), preferred_element_type=jnp.float32
    )
    gram_matrix = lax.psum(own_gram, "band")
    arrived = lax.all_gather(chosen, "band", axis=0, tiled=True)
    far_sum = jnp.dot(masked, arrived, preferred_element_type=jnp.float32)
    lower_factor = jnp.linalg.cholesky(gram_matrix)
    inverse = jax.scipy.linalg.cho_solve(
        (lower_factor, True), jnp.eye(rank_width, dtype=jnp.float32)
    )
    return jnp.dot(near_sum + far_sum, inverse, precision=lax.Precision.HIGHEST)


def solution(mesh):
    placed = (
        P(("groups", "band"), None),
        P(("groups", "band"), None, None, None),
        P(("groups", "band"), None),
        P(("groups", "band"), None),
        P(("groups", "band"), None),
    )
    return jax.shard_map(
        shards, mesh=mesh, in_specs=placed, out_specs=P(("groups", "band"), None), check_vma=False
    )
```

profile of v0, /device:TPU:0, one launch (start us, length us, event | category | flops | bytes accessed | tf_op | source)
XLA Modules:
  0.0 137.6 jit_solution(12282025486069231995)
XLA Ops:
  6.5 0.8 fusion.33
  7.4 2.3 %collective-permute-start = (bf16[128,128]{1,0:T(8,128)(2,1)S(1)}, bf16[128,128]{1,0:T(8,128)(2,1)S(1)}, u32[]{:S(2)}, u32[]{:S(2)}) collective-permute-start(bf16[128,128]{1,0:T(8,128)(2,1)S(1)} %get-tuple-element.11), channel_id=1, source_target_pairs={{0,1},{1,2},{2,3},{3,4},{4,5},{5,6},{6,7},{7,8},{8,9},{9,10},{10,1... | collective-permute-start | bytes 98312 | tf_op jit(solution)/shard_map/ppermute | solution.py:17
  9.7 1.3 collective-permute-start.1
  11.0 1.9 %fusion.34 = f32[128,128]{0,1:T(8,128)} fusion(bf16[1024,128]{1,0:T(8,128)(2,1)} %param.5), kind=kOutput, calls=%fused_computation.56 | convolution fusion | flops 33554432 | bytes 327680 | tf_op jit(solution)/shard_map/dot_general | solution.py:44
  13.0 0.7 fusion.29
  13.7 0.7 compare_and_fusion
  14.3 1.6 %gather_fusion = bf16[32,128]{1,0:T(8,128)(2,1)S(1)} fusion(bf16[1024,128]{1,0:T(8,128)(2,1)} %param.5, s32[1024]{0:T(1024)S(1)} %pad_clamp_fusion), kind=kCustom, calls=%fused_computation | custom fusion | bytes 16512 | tf_op jit(solution)/shard_map/jit(_take)/gather | solution.py:40
  15.9 0.7 broadcast_in_dim.28
  16.7 1.3 fusion.9
  18.1 26.7 %all_gather.3 = bf16[512,128]{1,0:T(8,128)(2,1)} all-gather(bf16[32,128]{1,0:T(8,128)(2,1)S(1)} %broadcast_select_fusion), channel_id=1, replica_groups=mesh['groups'=2,'band'=16] {'band'}, dimensions={0}, use_global_device_ids=true | all-gather | bytes 139264 | tf_op jit(solution)/shard_map/all_gather | solution.py:48
  45.5 56.8 %all-reduce.2.cloned.1.call-done = f32[128,128]{0,1:T(8,128)} async-done(((f32[128,128]{0,1:T(8,128)}), f32[128,128]{0,1:T(8,128)}) %all-reduce.2.cloned.1.call-update) | async-done | bytes 65552 | tf_op jit(solution)/shard_map/psum | solution.py:47
  102.3 0.9 copy.12
  103.2 0.9 fusion.24
  104.1 11.7 %cholesky.17 = f32[128,128]{1,0:T(8,128)S(1)} custom-call(f32[128,128]{1,0:T(8,128)S(1)} %fusion.24), custom_call_target="Cholesky" | custom-call | tf_op jit(solution)/shard_map/jit(cholesky)/cholesky | solution.py:50
  115.8 0.6 compare_reduce_fusion
  116.5 0.7 fusion.19
  117.1 9.8 %custom-call.10 = f32[1,128,128]{1,2,0:T(8,128)S(1)} custom-call(f32[1,128,128]{2,1,0:T(8,128)S(1)} %fusion.19), custom_call_target="InvertDiagBlocksLowerTriangular" | custom-call | tf_op jit(solution)/shard_map/jit(_cho_solve)/triangular_solve | solution.py:51
  127.0 0.2 fusion.22
  127.4 0.2 fusion.3
  127.7 0.2 fusion.1
  127.9 0.7 copy-done.2
  128.5 0.4 copy-done.3
  128.9 0.4 convolution_add_fusion
  129.4 1.4 fusion.35
  (23 shorter events, 1.0 us)
Async XLA Ops:
  6.5 38.3 %copy-start = (bf16[1024,128]{1,0:T(8,128)(2,1)S(1)}, bf16[1024,128]{1,0:T(8,128)(2,1)}, u32[]{:S(2)}) copy-start(bf16[1024,128]{1,0:T(8,128)(2,1)} %param.5) | copy-start | bytes 786436
  6.5 95.8 %all-reduce.2.cloned.1.call-start = ((), (), s32[]{:S(2)}) async-start(), calls=%async_computation | async-start | bytes 131072 | tf_op jit(solution)/shard_map/psum | solution.py:47
  7.4 37.5 %collective-permute-start = (bf16[128,128]{1,0:T(8,128)(2,1)S(1)}, bf16[128,128]{1,0:T(8,128)(2,1)S(1)}, u32[]{:S(2)}, u32[]{:S(2)}) collective-permute-start(bf16[128,128]{1,0:T(8,128)(2,1)S(1)} %get-tuple-element.11), channel_id=1, source_target_pairs={{0,1},{1,2},{2,3},{3,4},{4,5},{5,6},{6,7},{7,8},{8,9},{9,10},{10,1... | collective-permute-start | bytes 98312 | tf_op jit(solution)/shard_map/ppermute | solution.py:17
  9.7 35.5 %collective-permute-start.1 = (bf16[128,128]{1,0:T(8,128)(2,1)S(1)}, bf16[128,128]{1,0:T(8,128)(2,1)S(1)}, u32[]{:S(2)}, u32[]{:S(2)}) collective-permute-start(bf16[128,128]{1,0:T(8,128)(2,1)S(1)} %get-tuple-element.12), channel_id=1, source_target_pairs={{1,0},{2,1},{3,2},{4,3},{5,4},{6,5},{7,6},{8,7},{9,8},{10,9},{11,1... | collective-permute-start | bytes 98312 | tf_op jit(solution)/shard_map/ppermute | solution.py:18
  16.7 28.3 %copy-start.1 = (bf16[16,5,64,64]{3,2,1,0:T(8,128)(2,1)S(1)}, bf16[16,5,64,64]{3,2,1,0:T(8,128)(2,1)}, u32[]{:S(2)}) copy-start(bf16[16,5,64,64]{3,2,1,0:T(8,128)(2,1)} %param.6) | copy-start | bytes 1966084
  127.6 0.9 copy-start.2
  127.7 1.3 copy-start.3
Sparse Core Ops, SparseCore 0:
  13.1 89.1 all-reduce.1
where the time goes:
time: 139 us; the launch traced here: 138 us
  waiting for transfers between devices  56.8 us (41%)
  blocking collectives  26.7 us (19%)
  other arithmetic  25.1 us (18%)
  between operations  13.5 us (10%)
  matrix products  6.39 us (5%)
  local copies, waits for them, and re-layouts  5.35 us (4%)
  starting transfers between devices  3.64 us (3%)
    psum x1, waiting for transfers between devices, shards(): gram_matrix = lax.psum(own_gram, 'band')  56.8 us
    all_gather x1, blocking collectives, shards(): arrived = lax.all_gather(chosen, 'band', axis=0, tiled=True)  26.7 us
    another operation x3, other arithmetic, shards(): lower_factor = jnp.linalg.cholesky(gram_matrix)  12.4 us
    another operation x2, other arithmetic, shards(): jax.scipy.linalg.cho_solve((lower_factor, True), jnp.eye(rank_width, dtyp...  10.5 us
  transfers between devices with their start and end apart: 3, of which 1 were waited for; matrix products, arithmetic and copies ran while one was open for 6% of the time, Pallas kernels for 0%

commit v1 on v0

v1 whole, which is shorter than its diff:
```python
import functools

import jax
import jax.numpy as jnp
from jax import lax
from jax.experimental import pallas as pl
from jax.experimental.pallas import tpu as pltpu
from jax.sharding import PartitionSpec as P

BLOCK = 64
HALF_BLOCKS = 2
MESH = pl.DeviceIdType.MESH
TILE = 256


def gather_sums(
    n, far_count, factor, pub, near_hbm, far_hbm, sums, gram_out,
    near, far, shares, parts, total, arrived, picked, before, after,
    local_sem, part_send, part_recv, total_send, total_recv,
    pick_send, pick_recv, edge_send, edge_recv,
):
    group, me = lax.axis_index("groups"), lax.axis_index("band")
    rows, rank = factor.shape
    slots = pub.shape[1]
    height = shares.shape[1]
    margin = HALF_BLOCKS * BLOCK
    block_count = rows // BLOCK

    def peer(step):
        return lax.rem(me + step, n)

    barrier = pltpu.get_barrier_semaphore()

    @pl.loop(1, n)
    def _(step):
        pl.semaphore_signal(
            barrier, inc=1, device_id=(group, peer(step)), device_id_type=MESH
        )

    near_copy = pltpu.make_async_copy(near_hbm, near, local_sem.at[0])
    far_copy = pltpu.make_async_copy(far_hbm, far, local_sem.at[1])
    near_copy.start()
    far_copy.start()

    own = lax.dot_general(
        factor[...], factor[...], (((0,), (0,)), ((), ())),
        preferred_element_type=jnp.float32,
    )
    for index in range(n):
        shares[index] = own[index * height : (index + 1) * height]
    parts[me] = shares[me]

    def part_copy(step):
        return pltpu.make_async_remote_copy(
            src_ref=shares.at[peer(step)], dst_ref=parts.at[me],
            send_sem=part_send.at[step], recv_sem=part_recv.at[step],
            device_id=(group, peer(step)), device_id_type=MESH,
        )

    def total_copy(step):
        return pltpu.make_async_remote_copy(
            src_ref=total.at[me], dst_ref=total.at[me],
            send_sem=total_send.at[step], recv_sem=total_recv.at[step],
            device_id=(group, peer(step)), device_id_type=MESH,
        )

    def pick_copy(step):
        return pltpu.make_async_remote_copy(
            src_ref=arrived.at[me], dst_ref=arrived.at[me],
            send_sem=pick_send.at[step], recv_sem=pick_recv.at[step],
            device_id=(group, peer(step)), device_id_type=MESH,
        )

    pl.semaphore_wait(barrier, n - 1)

    @pl.loop(1, n)
    def _(step):
        part_copy(step).start()

    hit = lax.broadcasted_iota(jnp.int32, (rows, slots), 0) == pub[...]
    chosen = lax.dot_general(
        hit.astype(jnp.float32).astype(jnp.bfloat16), factor[...],
        (((0,), (0,)), ((), ())), preferred_element_type=jnp.float32,
    )
    arrived[me] = chosen.astype(jnp.bfloat16)

    @pl.loop(1, n)
    def _(step):
        pick_copy(step).start()

    down = pltpu.make_async_remote_copy(
        src_ref=factor.at[pl.ds(rows - margin, margin)], dst_ref=before,
        send_sem=edge_send.at[0], recv_sem=edge_recv.at[0],
        device_id=(group, peer(1)), device_id_type=MESH,
    )
    up = pltpu.make_async_remote_copy(
        src_ref=factor.at[pl.ds(0, margin)], dst_ref=after,
        send_sem=edge_send.at[1], recv_sem=edge_recv.at[1],
        device_id=(group, peer(n - 1)), device_id_type=MESH,
    )
    down.start()
    up.start()

    near_copy.wait()

    def near_dot(index, offset, block):
        return jnp.dot(near[index, offset], block, preferred_element_type=jnp.float32)

    @pl.loop(HALF_BLOCKS, block_count - HALF_BLOCKS)
    def _(index):
        value = jnp.zeros((BLOCK, rank), jnp.float32)
        for offset in range(2 * HALF_BLOCKS + 1):
            start = pl.multiple_of((index + offset - HALF_BLOCKS) * BLOCK, BLOCK)
            value = value + near_dot(index, offset, factor[pl.ds(start, BLOCK), :])
        sums[pl.ds(pl.multiple_of(index * BLOCK, BLOCK), BLOCK), :] = value

    @pl.loop(1, n)
    def _(step):
        part_copy(step).wait()

    total[me] = jnp.sum(parts[...], axis=0)

    @pl.loop(1, n)
    def _(step):
        total_copy(step).start()

    down.wait()
    up.wait()
    none = jnp.zeros((margin, rank), jnp.bfloat16)
    first = jnp.where(me > 0, before[...], none)
    last = jnp.where(me < n - 1, after[...], none)

    def block_at(place):
        if place < 0:
            return first[margin + place * BLOCK : margin + (place + 1) * BLOCK]
        if place >= block_count:
            at = (place - block_count) * BLOCK
            return last[at : at + BLOCK]
        return factor[place * BLOCK : (place + 1) * BLOCK, :]

    for index in [*range(HALF_BLOCKS), *range(block_count - HALF_BLOCKS, block_count)]:
        value = jnp.zeros((BLOCK, rank), jnp.float32)
        for offset in range(2 * HALF_BLOCKS + 1):
            value = value + near_dot(index, offset, block_at(index + offset - HALF_BLOCKS))
        sums[index * BLOCK : (index + 1) * BLOCK, :] = value

    @pl.loop(1, n)
    def _(step):
        pick_copy(step).wait()

    slot = lax.broadcasted_iota(jnp.int32, (slots, rank), 0)

    @pl.loop(0, n)
    def _(band):
        live = jnp.where(slot < far_count[0, band], arrived[band].astype(jnp.float32), 0.0)
        at = pl.multiple_of(band * slots, slots)
        picked[pl.ds(at, slots), :] = live.astype(jnp.bfloat16)

    far_copy.wait()

    @pl.loop(0, rows // TILE)
    def _(tile):
        at = pl.ds(pl.multiple_of(tile * TILE, TILE), TILE)
        sums[at, :] += jnp.dot(far[at, :], picked[...], preferred_element_type=jnp.float32)

    @pl.loop(1, n)
    def _(step):
        total_copy(step).wait()

    gram_out[...] = total[...]


def solve(gram, sums, out):
    rank = gram.shape[0]
    slabs = [gram[8 * i : 8 * i + 8, :] for i in range(rank // 8)]
    lane = lax.broadcasted_iota(jnp.int32, (8, rank), 1)
    sub = lax.broadcasted_iota(jnp.int32, (8, rank), 0)
    for k in range(rank):
        home, s = divmod(k, 8)
        at_lane = lane == k
        row = jnp.broadcast_to(slabs[home][s : s + 1, :], (8, rank))
        inv = 1.0 / jnp.broadcast_to(slabs[home][s : s + 1, k : k + 1], (8, rank))
        scaled = jnp.where(at_lane, inv, row * inv)
        new = []
        for i, slab in enumerate(slabs):
            col = jnp.broadcast_to(slab[:, k : k + 1], (8, rank))
            value = jnp.where(at_lane, 0.0, slab) - col * scaled
            if i == home:
                value = jnp.where(sub == s, scaled, value)
            new.append(value)
        slabs = new
    inverse = jnp.concatenate(slabs, axis=0)
    out[...] = jnp.dot(
        sums[...], inverse, precision=lax.Precision.HIGHEST,
        preferred_element_type=jnp.float32,
    )


def shards(factor, near_vals, far_vals, pub_rows, far_count):
    n = lax.axis_size("band")
    rows, rank = factor.shape
    slots = pub_rows.shape[1]
    height = rank // n
    margin = HALF_BLOCKS * BLOCK
    vmem = pl.BlockSpec(memory_space=pltpu.VMEM)
    anywhere = pl.BlockSpec(memory_space=pl.ANY)
    dma = pltpu.SemaphoreType.DMA
    sums, gram = pl.pallas_call(
        functools.partial(gather_sums, n),
        out_shape=(
            jax.ShapeDtypeStruct((rows, rank), jnp.float32),
            jax.ShapeDtypeStruct((n, height, rank), jnp.float32),
        ),
        in_specs=[pl.BlockSpec(memory_space=pltpu.SMEM), vmem, vmem, anywhere, anywhere],
        out_specs=(vmem, vmem),
        scratch_shapes=[
            pltpu.VMEM(near_vals.shape, jnp.bfloat16),
            pltpu.VMEM(far_vals.shape, jnp.bfloat16),
            pltpu.VMEM((n, height, rank), jnp.float32),
            pltpu.VMEM((n, height, rank), jnp.float32),
            pltpu.VMEM((n, height, rank), jnp.float32),
            pltpu.VMEM((n, slots, rank), jnp.bfloat16),
            pltpu.VMEM((n * slots, rank), jnp.bfloat16),
            pltpu.VMEM((margin, rank), jnp.bfloat16),
            pltpu.VMEM((margin, rank), jnp.bfloat16),
            dma((2,)),
            dma((n,)), dma((n,)), dma((n,)), dma((n,)), dma((n,)), dma((n,)),
            dma((2,)), dma((2,)),
        ],
        compiler_params=pltpu.CompilerParams(
            collective_id=0, has_side_effects=True, vmem_limit_bytes=48 << 20
        ),
    )(far_count, factor, pub_rows, near_vals, far_vals)
    return pl.pallas_call(
        solve,
        out_shape=jax.ShapeDtypeStruct((rows, rank), jnp.float32),
        in_specs=[vmem, vmem],
        out_specs=vmem,
        compiler_params=pltpu.CompilerParams(vmem_limit_bytes=32 << 20),
    )(gram.reshape(rank, rank), sums)


def solution(mesh):
    placed = (
        P(("groups", "band"), None),
        P(("groups", "band"), None, None, None),
        P(("groups", "band"), None),
        P(("groups", "band"), None),
        P(("groups", "band"), None),
    )
    return jax.shard_map(
        shards, mesh=mesh, in_specs=placed, out_specs=P(("groups", "band"), None), check_vma=False
    )
```

time: 139 us -> 40.2 us (0.29)
  waiting for transfers between devices: 56.8 us -> 0 us
  Pallas kernels: 0 us -> 35.1 us
  blocking collectives: 26.7 us -> 0 us
  other arithmetic: 25.1 us -> 0 us
  between operations: 13.5 us -> 0.01 us
  matrix products: 6.39 us -> 0 us
  starting transfers between devices: 3.64 us -> 0 us
    psum x1 -> x0, waiting for transfers between devices: 56.8 us -> none  [shards(): gram_matrix = lax.psum(own_gram, 'band')]
    pallas_call x0 -> x2, Pallas kernels: none -> 35.1 us  [the longest x1 18.8 us: shards(): pl.pallas_call(solve, out_shape=jax.ShapeDtypeStruct((rows, rank), jnp.fl...]
    all_gather x1 -> x0, blocking collectives: 26.7 us -> none  [shards(): arrived = lax.all_gather(chosen, 'band', axis=0, tiled=True)]
    another operation x5 -> x0, other arithmetic: 22.9 us -> none  [the longest x3 12.4 us: shards(): lower_factor = jnp.linalg.cholesky(gram_matrix)]
    dot_general x8 -> x0, matrix products: 5.93 us -> none  [the longest x5 2.2 us: shards(): jnp.einsum('bij,bjk->bik', near_vals[:, offset], blocks[offset:offset + b...]
    unnamed x9 -> x10, local copies, waits for them, and re-layouts: 1.08 us -> 4.8 us
    ppermute x2 -> x0, starting transfers between devices: 3.64 us -> none  [the longest x1 2.35 us: extended(): before = lax.ppermute(last, axis, up)]
    gather x1 -> x0, local copies, waits for them, and re-layouts: 1.56 us -> none  [shards(): chosen = jnp.take(factor, pub_rows[0], axis=0)]
  transfers between devices with their start and end apart: 3 -> 0, of which waited for: 1 -> 0; matrix products, arithmetic and copies ran while one was open for 6% -> 0% of each run, Pallas kernels for 0% -> 0%
where the time goes in v1:
time: 40.2 us; the launch traced here: 39.9 us
  Pallas kernels  35.1 us (87%)
  local copies, waits for them, and re-layouts  4.8 us (12%)
    pallas_call x1, Pallas kernels, shards(): pl.pallas_call(solve, out_shape=jax.ShapeDtypeStruct((rows, rank), jnp.fl...  18.8 us
    pallas_call x1, Pallas kernels, shards(): pl.pallas_call(functools.partial(gather_sums, n), out_shape=(jax.ShapeDty...  16.3 us
    unnamed x10, local copies, waits for them, and re-layouts  4.8 us

profile of v1, /device:TPU:0, one launch (start us, length us, event | category | flops | bytes accessed | tf_op | source)
XLA Modules:
  0.0 39.9 jit_solution(5844951182798636612)
XLA Ops:
  0.0 0.0 copy-start
  0.0 1.3 %copy-done = bf16[16,5,64,64]{3,2,1,0:T(8,128)(2,1)S(1)} copy-done((bf16[16,5,64,64]{3,2,1,0:T(8,128)(2,1)S(1)}, bf16[16,5,64,64]{3,2,1,0:T(8,128)(2,1)}, u32[]{:S(2)}) %copy-start) | copy-done | bytes 655384
  1.3 0.0 copy-start.1
  1.3 1.2 %copy-done.1 = bf16[1024,512]{1,0:T(8,128)(2,1)S(1)} copy-done((bf16[1024,512]{1,0:T(8,128)(2,1)S(1)}, bf16[1024,512]{1,0:T(8,128)(2,1)}, u32[]{:S(2)}) %copy-start.1) | copy-done | bytes 1048600
  2.5 0.0 copy-start.2
  2.5 0.9 %copy-done.2 = bf16[1024,128]{1,0:T(8,128)(2,1)S(1)} copy-done((bf16[1024,128]{1,0:T(8,128)(2,1)S(1)}, bf16[1024,128]{1,0:T(8,128)(2,1)}, u32[]{:S(2)}) %copy-start.2) | copy-done | bytes 262168
  3.5 0.0 copy-start.3
  3.5 0.7 %copy-done.3 = s32[1,16]{1,0:T(1,128)S(1)} copy-done((s32[1,16]{1,0:T(1,128)S(1)}, s32[1,16]{1,0:T(1,128)}, u32[]{:S(2)}) %copy-start.3) | copy-done | bytes 88
  4.1 0.0 copy-start.4
  4.2 0.7 %copy-done.4 = s32[1,32]{1,0:T(1,128)S(1)} copy-done((s32[1,32]{1,0:T(1,128)S(1)}, s32[1,32]{1,0:T(1,128)}, u32[]{:S(2)}) %copy-start.4) | copy-done | bytes 152
  4.8 16.3 %shard_map.55 = (f32[1024,128]{1,0:T(8,128)S(1)}, f32[16,8,128]{2,1,0:T(8,128)S(1)}) custom-call(s32[1,16]{1,0:T(1,128)S(1)} %copy-done.3, bf16[1024,128]{1,0:T(8,128)(2,1)S(1)} %copy-done.2, s32[1,32]{1,0:T(1,128)S(1)} %copy-done.4, bf16[16,5,64,64]{3,2,1,0:T(8,128)(2,1)S(1)} %copy-done, bf16[1024,512]{1,0:T(8,128)(2,1)S(1)} %copy-done.1), custom_call_target="tpu_custom_call" | custom-call | tf_op jit(solution)/shard_map/pallas_call | solution.py:208
  21.2 18.8 %shard_map.56 = f32[1024,128]{1,0:T(8,128)} custom-call(f32[128,128]{1,0:T(8,128)S(1)} %bitcast.1, f32[1024,128]{1,0:T(8,128)S(1)} %get-tuple-element.8.sums), custom_call_target="tpu_custom_call" | custom-call | tf_op jit(solution)/shard_map/pallas_call | solution.py:234
Async XLA Ops:
  0.0 1.3 %copy-start = (bf16[16,5,64,64]{3,2,1,0:T(8,128)(2,1)S(1)}, bf16[16,5,64,64]{3,2,1,0:T(8,128)(2,1)}, u32[]{:S(2)}) copy-start(bf16[16,5,64,64]{3,2,1,0:T(8,128)(2,1)} %near_hbm.1) | copy-start | bytes 1966084
  1.3 1.2 %copy-start.1 = (bf16[1024,512]{1,0:T(8,128)(2,1)S(1)}, bf16[1024,512]{1,0:T(8,128)(2,1)}, u32[]{:S(2)}) copy-start(bf16[1024,512]{1,0:T(8,128)(2,1)} %far_hbm.1) | copy-start | bytes 3145732
  2.5 0.9 %copy-start.2 = (bf16[1024,128]{1,0:T(8,128)(2,1)S(1)}, bf16[1024,128]{1,0:T(8,128)(2,1)}, u32[]{:S(2)}) copy-start(bf16[1024,128]{1,0:T(8,128)(2,1)} %factor.1) | copy-start | bytes 786436
  3.5 0.7 %copy-start.3 = (s32[1,16]{1,0:T(1,128)S(1)}, s32[1,16]{1,0:T(1,128)}, u32[]{:S(2)}) copy-start(s32[1,16]{1,0:T(1,128)} %far_count.1) | copy-start | bytes 196
  4.1 0.7 %copy-start.4 = (s32[1,32]{1,0:T(1,128)S(1)}, s32[1,32]{1,0:T(1,128)}, u32[]{:S(2)}) copy-start(s32[1,32]{1,0:T(1,128)} %pub.1) | copy-start | bytes 388

commit v2 on v1

--- a/solution.py
+++ b/solution.py
@@ -14,8 +14,8 @@
 
 
 def gather_sums(
-    n, far_count, factor, pub, near_hbm, far_hbm, sums, gram_out,
-    near, far, shares, parts, total, arrived, picked, before, after,
+    n, count_hbm, factor_hbm, pub_hbm, near_hbm, far_hbm, sums, gram_out,
+    far_count, factor, pub, near, far, shares, parts, total, arrived, picked, before, after,
     local_sem, part_send, part_recv, total_send, total_recv,
     pick_send, pick_recv, edge_send, edge_recv,
 ):
@@ -39,8 +39,15 @@
 
     near_copy = pltpu.make_async_copy(near_hbm, near, local_sem.at[0])
     far_copy = pltpu.make_async_copy(far_hbm, far, local_sem.at[1])
+    factor_copy = pltpu.make_async_copy(factor_hbm, factor, local_sem.at[2])
+    pub_copy = pltpu.make_async_copy(pub_hbm, pub, local_sem.at[3])
+    count_copy = pltpu.make_async_copy(count_hbm, far_count, local_sem.at[4])
+    factor_copy.start()
+    pub_copy.start()
+    count_copy.start()
     near_copy.start()
     far_copy.start()
+    factor_copy.wait()
 
     own = lax.dot_general(
         factor[...], factor[...], (((0,), (0,)), ((), ())),
@@ -77,6 +84,7 @@
     def _(step):
         part_copy(step).start()
 
+    pub_copy.wait()
     hit = lax.broadcasted_iota(jnp.int32, (rows, slots), 0) == pub[...]
     chosen = lax.dot_general(
         hit.astype(jnp.float32).astype(jnp.bfloat16), factor[...],
@@ -148,6 +156,7 @@
     def _(step):
         pick_copy(step).wait()
 
+    count_copy.wait()
     slot = lax.broadcasted_iota(jnp.int32, (slots, rank), 0)
 
     @pl.loop(0, n)
@@ -170,30 +179,50 @@
     gram_out[...] = total[...]
 
 
-def solve(gram, sums, out):
+def solve(gram, sums, out, inverse):
+    @pl.when(pl.program_id(0) == 0)
+    def _():
+        inverse[...] = inverted(gram)
+
+    out[...] = jnp.dot(
+        sums[...], inverse[...], precision=lax.Precision.HIGHEST,
+        preferred_element_type=jnp.float32,
+    )
+
+
+def inverted(gram):
     rank = gram.shape[0]
     slabs = [gram[8 * i : 8 * i + 8, :] for i in range(rank // 8)]
     lane = lax.broadcasted_iota(jnp.int32, (8, rank), 1)
     sub = lax.broadcasted_iota(jnp.int32, (8, rank), 0)
-    for k in range(rank):
-        home, s = divmod(k, 8)
-        at_lane = lane == k
-        row = jnp.broadcast_to(slabs[home][s : s + 1, :], (8, rank))
-        inv = 1.0 / jnp.broadcast_to(slabs[home][s : s + 1, k : k + 1], (8, rank))
-        scaled = jnp.where(at_lane, inv, row * inv)
+    for home in range(rank // 8):
+        base = 8 * home
+        panel = slabs[home]
+        spread = [
+            jnp.broadcast_to(panel[:, base + j : base + j + 1], (8, rank)) for j in range(8)
+        ]
+        for j in range(8):
+            inv = 1.0 / jnp.broadcast_to(spread[j][j : j + 1, :], (8, rank))
+            row = jnp.broadcast_to(panel[j : j + 1, :], (8, rank)) * inv
+            at_lane, at_row = lane == base + j, sub == j
+            scaled = jnp.where(at_lane, inv, row)
+            panel = jnp.where(
+                at_row, scaled, jnp.where(at_lane, 0.0, panel) - spread[j] * scaled
+            )
+            for l in range(j + 1, 8):
+                ahead = jnp.broadcast_to(spread[l][j : j + 1, :], (8, rank)) * inv
+                spread[l] = jnp.where(at_row, ahead, spread[l] - spread[j] * ahead)
+        in_block = (lane >= base) & (lane < base + 8)
+        rows = [jnp.broadcast_to(panel[j : j + 1, :], (8, rank)) for j in range(8)]
         new = []
         for i, slab in enumerate(slabs):
-            col = jnp.broadcast_to(slab[:, k : k + 1], (8, rank))
-            value = jnp.where(at_lane, 0.0, slab) - col * scaled
-            if i == home:
-                value = jnp.where(sub == s, scaled, value)
-            new.append(value)
+            value = jnp.where(in_block, 0.0, slab)
+            for j in range(8):
+                col = jnp.broadcast_to(slab[:, base + j : base + j + 1], (8, rank))
+                value = value - col * rows[j]
+            new.append(panel if i == home else value)
         slabs = new
-    inverse = jnp.concatenate(slabs, axis=0)
-    out[...] = jnp.dot(
-        sums[...], inverse, precision=lax.Precision.HIGHEST,
-        preferred_element_type=jnp.float32,
-    )
+    return jnp.concatenate(slabs, axis=0)
 
 
 def shards(factor, near_vals, far_vals, pub_rows, far_count):
@@ -203,7 +232,7 @@
     height = rank // n
     margin = HALF_BLOCKS * BLOCK
     vmem = pl.BlockSpec(memory_space=pltpu.VMEM)
-    anywhere = pl.BlockSpec(memory_space=pl.ANY)
+    anywhere = pl.BlockSpec(memory_space=pltpu.HBM)
     dma = pltpu.SemaphoreType.DMA
     sums, gram = pl.pallas_call(
         functools.partial(gather_sums, n),
@@ -211,9 +240,12 @@
             jax.ShapeDtypeStruct((rows, rank), jnp.float32),
             jax.ShapeDtypeStruct((n, height, rank), jnp.float32),
         ),
-        in_specs=[pl.BlockSpec(memory_space=pltpu.SMEM), vmem, vmem, anywhere, anywhere],
+        in_specs=[anywhere] * 5,
         out_specs=(vmem, vmem),
         scratch_shapes=[
+            pltpu.SMEM(far_count.shape, jnp.int32),
+            pltpu.VMEM(factor.shape, jnp.bfloat16),
+            pltpu.VMEM(pub_rows.shape, jnp.int32),
             pltpu.VMEM(near_vals.shape, jnp.bfloat16),
             pltpu.VMEM(far_vals.shape, jnp.bfloat16),
             pltpu.VMEM((n, height, rank), jnp.float32),
@@ -223,20 +255,25 @@
             pltpu.VMEM((n * slots, rank), jnp.bfloat16),
             pltpu.VMEM((margin, rank), jnp.bfloat16),
             pltpu.VMEM((margin, rank), jnp.bfloat16),
-            dma((2,)),
+            dma((5,)),
             dma((n,)), dma((n,)), dma((n,)), dma((n,)), dma((n,)), dma((n,)),
             dma((2,)), dma((2,)),
         ],
         compiler_params=pltpu.CompilerParams(
-            collective_id=0, has_side_effects=True, vmem_limit_bytes=48 << 20
+            collective_id=0, has_side_effects=True, vmem_limit_bytes=60 << 20
         ),
     )(far_count, factor, pub_rows, near_vals, far_vals)
     return pl.pallas_call(
         solve,
         out_shape=jax.ShapeDtypeStruct((rows, rank), jnp.float32),
-        in_specs=[vmem, vmem],
-        out_specs=vmem,
-        compiler_params=pltpu.CompilerParams(vmem_limit_bytes=32 << 20),
+        grid=(rows // TILE,),
+        in_specs=[
+            pl.BlockSpec((rank, rank), lambda i: (0, 0)),
+            pl.BlockSpec((TILE, rank), lambda i: (i, 0)),
+        ],
+        out_specs=pl.BlockSpec((TILE, rank), lambda i: (i, 0)),
+        scratch_shapes=[pltpu.VMEM((rank, rank), jnp.float32)],
+        compiler_params=pltpu.CompilerParams(vmem_limit_bytes=60 << 20),
     )(gram.reshape(rank, rank), sums)
 
 

time: 40.2 us -> 24.6 us (0.61)
  Pallas kernels: 35.1 us -> 24.4 us
  local copies, waits for them, and re-layouts: 4.8 us -> 0 us
    pallas_call x1, Pallas kernels: 18.8 us -> 7.8 us  [shards(): pl.pallas_call(solve, out_shape=jax.ShapeDtypeStruct((rows, rank), jnp.fl...]
    unnamed x10 -> x0, local copies, waits for them, and re-layouts: 4.8 us -> none
where the time goes in v2:
time: 24.6 us; the launch traced here: 24.4 us
  Pallas kernels  24.4 us (99%)
    pallas_call x1, Pallas kernels, shards(): pl.pallas_call(functools.partial(gather_sums, n), out_shape=(jax.ShapeDty...  16.6 us
    pallas_call x1, Pallas kernels, shards(): pl.pallas_call(solve, out_shape=jax.ShapeDtypeStruct((rows, rank), jnp.fl...  7.8 us

profile of v2, /device:TPU:0, one launch (start us, length us, event | category | flops | bytes accessed | tf_op | source)
XLA Modules:
  0.0 24.4 jit_solution(15208854063012492299)
XLA Ops:
  0.0 16.6 %shard_map.55 = (f32[1024,128]{1,0:T(8,128)}, f32[16,8,128]{2,1,0:T(8,128)}) custom-call(s32[1,16]{1,0:T(1,128)} %count_hbm.1, bf16[1024,128]{1,0:T(8,128)(2,1)} %factor_hbm.1, s32[1,32]{1,0:T(1,128)} %pub_hbm.1, bf16[16,5,64,64]{3,2,1,0:T(8,128)(2,1)} %near_hbm.1, bf16[1024,512]{1,0:T(8,128)(2,1)} %far_hbm.1), custom_call_target="tpu_custom_call" | custom-call | tf_op jit(solution)/shard_map/pallas_call | solution.py:237
  16.6 7.8 %shard_map.56 = f32[1024,128]{1,0:T(8,128)} custom-call(f32[128,128]{1,0:T(8,128)} %bitcast.1, f32[1024,128]{1,0:T(8,128)} %get-tuple-element.8.sums), custom_call_target="tpu_custom_call" | custom-call | tf_op jit(solution)/shard_map/pallas_call | solution.py:266

commit v3 on v2

--- a/solution.py
+++ b/solution.py
@@ -10,13 +10,13 @@
 BLOCK = 64
 HALF_BLOCKS = 2
 MESH = pl.DeviceIdType.MESH
-TILE = 256
+TILE = 512
 
 
 def gather_sums(
-    n, count_hbm, factor_hbm, pub_hbm, near_hbm, far_hbm, sums, gram_out,
-    far_count, factor, pub, near, far, shares, parts, total, arrived, picked, before, after,
-    local_sem, part_send, part_recv, total_send, total_recv,
+    n, near_n, count_hbm, factor_hbm, pub_hbm, near_hbm, far_hbm, sums_hbm, gram_out,
+    sums, far_count, factor, pub, near, far, shares, parts, cross, total, arrived, picked, before, after,
+    local_sem, part_send, part_recv, cross_send, cross_recv, total_send, total_recv,
     pick_send, pick_recv, edge_send, edge_recv,
 ):
     group, me = lax.axis_index("groups"), lax.axis_index("band")
@@ -26,8 +26,14 @@
     margin = HALF_BLOCKS * BLOCK
     block_count = rows // BLOCK
 
+    far_n = n // near_n
+    inner, outer = lax.rem(me, near_n), lax.div(me, near_n)
+
     def peer(step):
         return lax.rem(me + step, n)
+
+    def beside(step):
+        return lax.rem(inner + step, near_n)
 
     barrier = pltpu.get_barrier_semaphore()
 
@@ -53,22 +59,29 @@
         factor[...], factor[...], (((0,), (0,)), ((), ())),
         preferred_element_type=jnp.float32,
     )
-    for index in range(n):
+    for index in range(near_n):
         shares[index] = own[index * height : (index + 1) * height]
-    parts[me] = shares[me]
+    parts[inner] = shares[inner]
 
     def part_copy(step):
         return pltpu.make_async_remote_copy(
-            src_ref=shares.at[peer(step)], dst_ref=parts.at[me],
+            src_ref=shares.at[beside(step)], dst_ref=parts.at[inner],
             send_sem=part_send.at[step], recv_sem=part_recv.at[step],
-            device_id=(group, peer(step)), device_id_type=MESH,
+            device_id=(group, outer * near_n + beside(step)), device_id_type=MESH,
+        )
+
+    def cross_copy(step):
+        return pltpu.make_async_remote_copy(
+            src_ref=cross.at[outer], dst_ref=cross.at[outer],
+            send_sem=cross_send.at[step], recv_sem=cross_recv.at[step],
+            device_id=(group, peer(step * near_n)), device_id_type=MESH,
         )
 
     def total_copy(step):
         return pltpu.make_async_remote_copy(
-            src_ref=total.at[me], dst_ref=total.at[me],
+            src_ref=total.at[inner], dst_ref=total.at[inner],
             send_sem=total_send.at[step], recv_sem=total_recv.at[step],
-            device_id=(group, peer(step)), device_id_type=MESH,
+            device_id=(group, outer * near_n + beside(step)), device_id_type=MESH,
         )
 
     def pick_copy(step):
@@ -80,8 +93,7 @@
 
     pl.semaphore_wait(barrier, n - 1)
 
-    @pl.loop(1, n)
-    def _(step):
+    for step in range(1, near_n):
         part_copy(step).start()
 
     pub_copy.wait()
@@ -108,6 +120,13 @@
     )
     down.start()
     up.start()
+
+    for step in range(1, near_n):
+        part_copy(step).wait()
+
+    cross[outer] = jnp.sum(parts[...], axis=0)
+    for step in range(1, far_n):
+        cross_copy(step).start()
 
     near_copy.wait()
 
@@ -122,14 +141,12 @@
             value = value + near_dot(index, offset, factor[pl.ds(start, BLOCK), :])
         sums[pl.ds(pl.multiple_of(index * BLOCK, BLOCK), BLOCK), :] = value
 
-    @pl.loop(1, n)
-    def _(step):
-        part_copy(step).wait()
-
-    total[me] = jnp.sum(parts[...], axis=0)
-
-    @pl.loop(1, n)
-    def _(step):
+    for step in range(1, far_n):
+        cross_copy(step).wait()
+
+    total[inner] = jnp.sum(cross[...], axis=0)
+
+    for step in range(1, near_n):
         total_copy(step).start()
 
     down.wait()
@@ -172,10 +189,13 @@
         at = pl.ds(pl.multiple_of(tile * TILE, TILE), TILE)
         sums[at, :] += jnp.dot(far[at, :], picked[...], preferred_element_type=jnp.float32)
 
-    @pl.loop(1, n)
-    def _(step):
+    sums_copy = pltpu.make_async_copy(sums, sums_hbm, local_sem.at[5])
+    sums_copy.start()
+
+    for step in range(1, near_n):
         total_copy(step).wait()
 
+    sums_copy.wait()
     gram_out[...] = total[...]
 
 
@@ -229,34 +249,40 @@
     n = lax.axis_size("band")
     rows, rank = factor.shape
     slots = pub_rows.shape[1]
-    height = rank // n
+    near_n = 1
+    while 4 * near_n * near_n <= n:
+        near_n *= 2
+    height = rank // near_n
     margin = HALF_BLOCKS * BLOCK
     vmem = pl.BlockSpec(memory_space=pltpu.VMEM)
     anywhere = pl.BlockSpec(memory_space=pltpu.HBM)
     dma = pltpu.SemaphoreType.DMA
     sums, gram = pl.pallas_call(
-        functools.partial(gather_sums, n),
+        functools.partial(gather_sums, n, near_n),
         out_shape=(
             jax.ShapeDtypeStruct((rows, rank), jnp.float32),
-            jax.ShapeDtypeStruct((n, height, rank), jnp.float32),
+            jax.ShapeDtypeStruct((near_n, height, rank), jnp.float32),
         ),
         in_specs=[anywhere] * 5,
-        out_specs=(vmem, vmem),
+        out_specs=(anywhere, vmem),
         scratch_shapes=[
+            pltpu.VMEM((rows, rank), jnp.float32),
             pltpu.SMEM(far_count.shape, jnp.int32),
             pltpu.VMEM(factor.shape, jnp.bfloat16),
             pltpu.VMEM(pub_rows.shape, jnp.int32),
             pltpu.VMEM(near_vals.shape, jnp.bfloat16),
             pltpu.VMEM(far_vals.shape, jnp.bfloat16),
-            pltpu.VMEM((n, height, rank), jnp.float32),
-            pltpu.VMEM((n, height, rank), jnp.float32),
-            pltpu.VMEM((n, height, rank), jnp.float32),
+            pltpu.VMEM((near_n, height, rank), jnp.float32),
+            pltpu.VMEM((near_n, height, rank), jnp.float32),
+            pltpu.VMEM((n // near_n, height, rank), jnp.float32),
+            pltpu.VMEM((near_n, height, rank), jnp.float32),
             pltpu.VMEM((n, slots, rank), jnp.bfloat16),
             pltpu.VMEM((n * slots, rank), jnp.bfloat16),
             pltpu.VMEM((margin, rank), jnp.bfloat16),
             pltpu.VMEM((margin, rank), jnp.bfloat16),
-            dma((5,)),
-            dma((n,)), dma((n,)), dma((n,)), dma((n,)), dma((n,)), dma((n,)),
+            dma((6,)),
+            dma((near_n,)), dma((near_n,)), dma((n // near_n,)), dma((n // near_n,)),
+            dma((near_n,)), dma((near_n,)), dma((n,)), dma((n,)),
             dma((2,)), dma((2,)),
         ],
         compiler_params=pltpu.CompilerParams(

time: 24.6 us -> 22.6 us (0.919)
  Pallas kernels: 24.4 us -> 22.5 us
    pallas_call x1, Pallas kernels: 7.8 us -> 6.56 us  [shards(): pl.pallas_call(solve, out_shape=jax.ShapeDtypeStruct((rows, rank), jnp.fl...]
    pallas_call x1, Pallas kernels: 16.6 us -> 15.9 us  [shards(): pl.pallas_call(functools.partial(gather_sums, n, near_n), out_shape=(jax....]
where the time goes in v3:
time: 22.6 us; the launch traced here: 22.5 us
  Pallas kernels  22.5 us (100%)
    pallas_call x1, Pallas kernels, shards(): pl.pallas_call(functools.partial(gather_sums, n, near_n), out_shape=(jax....  15.9 us
    pallas_call x1, Pallas kernels, shards(): pl.pallas_call(solve, out_shape=jax.ShapeDtypeStruct((rows, rank), jnp.fl...  6.56 us

profile of v3, /device:TPU:0, one launch (start us, length us, event | category | flops | bytes accessed | tf_op | source)
XLA Modules:
  0.0 22.5 jit_solution(1649777653042725062)
XLA Ops:
  0.0 15.9 %shard_map.55 = (f32[1024,128]{1,0:T(8,128)}, f32[4,32,128]{2,1,0:T(8,128)}) custom-call(s32[1,16]{1,0:T(1,128)} %count_hbm.1, bf16[1024,128]{1,0:T(8,128)(2,1)} %factor_hbm.1, s32[1,32]{1,0:T(1,128)} %pub_hbm.1, bf16[16,5,64,64]{3,2,1,0:T(8,128)(2,1)} %near_hbm.1, bf16[1024,512]{1,0:T(8,128)(2,1)} %far_hbm.1), custom_call_target="tpu_custom_call" | custom-call | tf_op jit(solution)/shard_map/pallas_call | solution.py:260
  15.9 6.6 %shard_map.56 = f32[1024,128]{1,0:T(8,128)} custom-call(f32[128,128]{1,0:T(8,128)} %bitcast.1, f32[1024,128]{1,0:T(8,128)} %get-tuple-element.8.sums), custom_call_target="tpu_custom_call" | custom-call | tf_op jit(solution)/shard_map/pallas_call | solution.py:292

commit v4 on v3

--- a/solution.py
+++ b/solution.py
@@ -17,7 +17,7 @@
     n, near_n, count_hbm, factor_hbm, pub_hbm, near_hbm, far_hbm, sums_hbm, gram_out,
     sums, far_count, factor, pub, near, far, shares, parts, cross, total, arrived, picked, before, after,
     local_sem, part_send, part_recv, cross_send, cross_recv, total_send, total_recv,
-    pick_send, pick_recv, edge_send, edge_recv,
+    pick_send, pick_recv, band_send, band_recv, edge_send, edge_recv,
 ):
     group, me = lax.axis_index("groups"), lax.axis_index("band")
     rows, rank = factor.shape
@@ -37,10 +37,12 @@
 
     barrier = pltpu.get_barrier_semaphore()
 
-    @pl.loop(1, n)
-    def _(step):
+    partners = [outer * near_n + beside(step) for step in range(1, near_n)]
+    partners += [peer(step * near_n) for step in range(1, far_n)]
+    partners += [peer(1), peer(n - 1)]
+    for partner in partners:
         pl.semaphore_signal(
-            barrier, inc=1, device_id=(group, peer(step)), device_id_type=MESH
+            barrier, inc=1, device_id=(group, partner), device_id_type=MESH
         )
 
     near_copy = pltpu.make_async_copy(near_hbm, near, local_sem.at[0])
@@ -85,13 +87,22 @@
         )
 
     def pick_copy(step):
-        return pltpu.make_async_remote_copy(
-            src_ref=arrived.at[me], dst_ref=arrived.at[me],
+        own_rows = arrived.at[inner, outer]
+        return pltpu.make_async_remote_copy(
+            src_ref=own_rows, dst_ref=own_rows,
             send_sem=pick_send.at[step], recv_sem=pick_recv.at[step],
-            device_id=(group, peer(step)), device_id_type=MESH,
-        )
-
-    pl.semaphore_wait(barrier, n - 1)
+            device_id=(group, peer(step * near_n)), device_id_type=MESH,
+        )
+
+    def band_copy(step):
+        held = arrived.at[inner]
+        return pltpu.make_async_remote_copy(
+            src_ref=held, dst_ref=held,
+            send_sem=band_send.at[step], recv_sem=band_recv.at[step],
+            device_id=(group, outer * near_n + beside(step)), device_id_type=MESH,
+        )
+
+    pl.semaphore_wait(barrier, len(partners))
 
     for step in range(1, near_n):
         part_copy(step).start()
@@ -102,10 +113,9 @@
         hit.astype(jnp.float32).astype(jnp.bfloat16), factor[...],
         (((0,), (0,)), ((), ())), preferred_element_type=jnp.float32,
     )
-    arrived[me] = chosen.astype(jnp.bfloat16)
-
-    @pl.loop(1, n)
-    def _(step):
+    arrived[inner, outer] = chosen.astype(jnp.bfloat16)
+
+    for step in range(1, far_n):
         pick_copy(step).start()
 
     down = pltpu.make_async_remote_copy(
@@ -127,6 +137,11 @@
     cross[outer] = jnp.sum(parts[...], axis=0)
     for step in range(1, far_n):
         cross_copy(step).start()
+
+    for step in range(1, far_n):
+        pick_copy(step).wait()
+    for step in range(1, near_n):
+        band_copy(step).start()
 
     near_copy.wait()
 
@@ -169,16 +184,15 @@
             value = value + near_dot(index, offset, block_at(index + offset - HALF_BLOCKS))
         sums[index * BLOCK : (index + 1) * BLOCK, :] = value
 
-    @pl.loop(1, n)
-    def _(step):
-        pick_copy(step).wait()
+    for step in range(1, near_n):
+        band_copy(step).wait()
 
     count_copy.wait()
     slot = lax.broadcasted_iota(jnp.int32, (slots, rank), 0)
 
     @pl.loop(0, n)
     def _(band):
-        live = jnp.where(slot < far_count[0, band], arrived[band].astype(jnp.float32), 0.0)
+        live = jnp.where(slot < far_count[0, band], arrived[lax.rem(band, near_n), lax.div(band, near_n)].astype(jnp.float32), 0.0)
         at = pl.multiple_of(band * slots, slots)
         picked[pl.ds(at, slots), :] = live.astype(jnp.bfloat16)
 
@@ -276,13 +290,14 @@
             pltpu.VMEM((near_n, height, rank), jnp.float32),
             pltpu.VMEM((n // near_n, height, rank), jnp.float32),
             pltpu.VMEM((near_n, height, rank), jnp.float32),
-            pltpu.VMEM((n, slots, rank), jnp.bfloat16),
+            pltpu.VMEM((near_n, n // near_n, slots, rank), jnp.bfloat16),
             pltpu.VMEM((n * slots, rank), jnp.bfloat16),
             pltpu.VMEM((margin, rank), jnp.bfloat16),
             pltpu.VMEM((margin, rank), jnp.bfloat16),
             dma((6,)),
             dma((near_n,)), dma((near_n,)), dma((n // near_n,)), dma((n // near_n,)),
-            dma((near_n,)), dma((near_n,)), dma((n,)), dma((n,)),
+            dma((near_n,)), dma((near_n,)), dma((n // near_n,)), dma((n // near_n,)),
+            dma((near_n,)), dma((near_n,)),
             dma((2,)), dma((2,)),
         ],
         compiler_params=pltpu.CompilerParams(

time: 22.6 us -> 21.8 us (0.965)
  Pallas kernels: 22.5 us -> 21.6 us
    pallas_call x1, Pallas kernels: 15.9 us -> 15 us  [shards(): pl.pallas_call(functools.partial(gather_sums, n, near_n), out_shape=(jax....]
where the time goes in v4:
time: 21.8 us; the launch traced here: 21.6 us
  Pallas kernels  21.6 us (99%)
    pallas_call x1, Pallas kernels, shards(): pl.pallas_call(functools.partial(gather_sums, n, near_n), out_shape=(jax....  15 us
    pallas_call x1, Pallas kernels, shards(): pl.pallas_call(solve, out_shape=jax.ShapeDtypeStruct((rows, rank), jnp.fl...  6.56 us

profile of v4, /device:TPU:0, one launch (start us, length us, event | category | flops | bytes accessed | tf_op | source)
XLA Modules:
  0.0 21.6 jit_solution(15704602568287682801)
XLA Ops:
  0.0 15.0 %shard_map.55 = (f32[1024,128]{1,0:T(8,128)}, f32[4,32,128]{2,1,0:T(8,128)}) custom-call(s32[1,16]{1,0:T(1,128)} %count_hbm.1, bf16[1024,128]{1,0:T(8,128)(2,1)} %factor_hbm.1, s32[1,32]{1,0:T(1,128)} %pub_hbm.1, bf16[16,5,64,64]{3,2,1,0:T(8,128)(2,1)} %near_hbm.1, bf16[1024,512]{1,0:T(8,128)(2,1)} %far_hbm.1), custom_call_target="tpu_custom_call" | custom-call | tf_op jit(solution)/shard_map/pallas_call | solution.py:274
  15.1 6.6 %shard_map.56 = f32[1024,128]{1,0:T(8,128)} custom-call(f32[128,128]{1,0:T(8,128)} %bitcast.1, f32[1024,128]{1,0:T(8,128)} %get-tuple-element.8.sums), custom_call_target="tpu_custom_call" | custom-call | tf_op jit(solution)/shard_map/pallas_call | solution.py:307

commit v5 on v4

--- a/solution.py
+++ b/solution.py
@@ -53,8 +53,6 @@
     factor_copy.start()
     pub_copy.start()
     count_copy.start()
-    near_copy.start()
-    far_copy.start()
     factor_copy.wait()
 
     own = lax.dot_general(
@@ -101,11 +99,6 @@
             send_sem=band_send.at[step], recv_sem=band_recv.at[step],
             device_id=(group, outer * near_n + beside(step)), device_id_type=MESH,
         )
-
-    pl.semaphore_wait(barrier, len(partners))
-
-    for step in range(1, near_n):
-        part_copy(step).start()
 
     pub_copy.wait()
     hit = lax.broadcasted_iota(jnp.int32, (rows, slots), 0) == pub[...]
@@ -115,6 +108,11 @@
     )
     arrived[inner, outer] = chosen.astype(jnp.bfloat16)
 
+    pl.semaphore_wait(barrier, len(partners))
+
+    for step in range(1, near_n):
+        part_copy(step).start()
+
     for step in range(1, far_n):
         pick_copy(step).start()
 
@@ -128,6 +126,8 @@
         send_sem=edge_send.at[1], recv_sem=edge_recv.at[1],
         device_id=(group, peer(n - 1)), device_id_type=MESH,
     )
+    near_copy.start()
+    far_copy.start()
     down.start()
     up.start()
 

time: 21.8 us -> 21.8 us (level)
  no operation moved by 1% of the time
where the time goes in v5:
time: 21.8 us; the launch traced here: 21.6 us
  Pallas kernels  21.6 us (99%)
    pallas_call x1, Pallas kernels, shards(): pl.pallas_call(functools.partial(gather_sums, n, near_n), out_shape=(jax....  15 us
    pallas_call x1, Pallas kernels, shards(): pl.pallas_call(solve, out_shape=jax.ShapeDtypeStruct((rows, rank), jnp.fl...  6.56 us

profile of v5, /device:TPU:0, one launch (start us, length us, event | category | flops | bytes accessed | tf_op | source)
XLA Modules:
  0.0 21.6 jit_solution(2244002316050274202)
XLA Ops:
  0.0 15.0 %shard_map.55 = (f32[1024,128]{1,0:T(8,128)}, f32[4,32,128]{2,1,0:T(8,128)}) custom-call(s32[1,16]{1,0:T(1,128)} %count_hbm.1, bf16[1024,128]{1,0:T(8,128)(2,1)} %factor_hbm.1, s32[1,32]{1,0:T(1,128)} %pub_hbm.1, bf16[16,5,64,64]{3,2,1,0:T(8,128)(2,1)} %near_hbm.1, bf16[1024,512]{1,0:T(8,128)(2,1)} %far_hbm.1), custom_call_target="tpu_custom_call" | custom-call | tf_op jit(solution)/shard_map/pallas_call | solution.py:274
  15.1 6.6 %shard_map.56 = f32[1024,128]{1,0:T(8,128)} custom-call(f32[128,128]{1,0:T(8,128)} %bitcast.1, f32[1024,128]{1,0:T(8,128)} %get-tuple-element.8.sums), custom_call_target="tpu_custom_call" | custom-call | tf_op jit(solution)/shard_map/pallas_call | solution.py:307
